TPU v7x, 32 devices: a whole 2x2x4 slice. The times are simulated.
32 devices in a mesh: client: 4 (over x, core), tp: 8 (over z, y).
Axes of the slice: x: 2, y: 2, z: 4, core: 2. Of those that a mesh axis runs over, the one named last changes fastest.
Arguments:
- inputs: bfloat16 [4, 128, 2048], P('client'), may hold values from -6 to 6
- targets: bfloat16 [4, 128, 2048], P('client'), may hold values from -6 to 6
- norm_gain: float32 [2048], replicated, may hold values from 0.1 to 1.9
- gate_weight: bfloat16 [2048, 4096], P(None, 'tp'), may hold values from -0.125 to 0.125
- up_weight: bfloat16 [2048, 4096], P(None, 'tp'), may hold values from -0.125 to 0.125
- down_weight: bfloat16 [4096, 2048], P('tp'), may hold values from -0.09375 to 0.09375
- overflow: int32 [4, 3, 8], P('client', None, 'tp'), may hold values 0 or 1
Outputs:
- gate_update: float32 [2048, 4096], P('client', 'tp')
- up_update: float32 [2048, 4096], P('client', 'tp')
- down_update: float32 [4096, 2048], P('tp', 'client')
- gain_update: float32 [2048], P('client')
All inputs are finite; a program needn't handle non-finite values. No bound on the sum of `overflow` on one device may be relied on, other than what follows from the above.
Results may differ from a plain program's by a relative error of at most 0.014.
Values may be sent and summed in bfloat16 or wider, within the bound.
A program may use at most 128 MiB of HBM per device.

v0:
```python
import math

import jax
import jax.numpy as jnp
from jax import lax
from jax.sharding import PartitionSpec as P

D = 2048
FF = 4096
STEPS = 3


def contract_rows(left, right):
    return lax.dot_general(
        left, right, (((0,), (0,)), ((), ())), preferred_element_type=jnp.float32
    )


def contract_cols(left, right):
    return lax.dot_general(
        left, right, (((1,), (1,)), ((), ())), preferred_element_type=jnp.float32
    )


def on_device(inputs, targets, norm_gain, gate_weight, up_weight, down_weight, overflow):
    limit = 0.5 * math.sqrt(3.0 * D * FF)
    activ = inputs[0].astype(jnp.float32)
    target_rows = targets[0]
    scaled = activ * lax.rsqrt(jnp.mean(activ * activ, axis=-1, keepdims=True) + 1e-05)
    gain_master = norm_gain
    gate_master = gate_weight.astype(jnp.float32)
    up_master = up_weight.astype(jnp.float32)
    down_master = down_weight.astype(jnp.float32)
    gate_total = jnp.zeros_like(gate_master)
    up_total = jnp.zeros_like(up_master)
    down_total = jnp.zeros_like(down_master)
    gain_total = jnp.zeros_like(gain_master)
    for local_step in range(STEPS):
        normed = (scaled * gain_master).astype(jnp.bfloat16)
        gate_copy = gate_master.astype(jnp.bfloat16)
        up_copy = up_master.astype(jnp.bfloat16)
        down_copy = down_master.astype(jnp.bfloat16)
        gate_act = jnp.dot(normed, gate_copy, preferred_element_type=jnp.float32)
        up_act = jnp.dot(normed, up_copy, preferred_element_type=jnp.float32)
        sig_gate = jax.nn.sigmoid(gate_act)
        silu_gate = gate_act * sig_gate
        hidden = (silu_gate * up_act).astype(jnp.bfloat16)
        partial_value = jnp.dot(hidden, down_copy, preferred_element_type=jnp.float32)
        summed = lax.psum(partial_value, "tp")
        outputs = activ + summed
        grad_out = (outputs - target_rows.astype(jnp.float32)).astype(jnp.bfloat16)
        grad_down = contract_rows(hidden, grad_out)
        grad_hidden = contract_cols(grad_out, down_copy)
        grad_gate_act = (
            grad_hidden * up_act * (sig_gate * (1.0 + gate_act * (1.0 - sig_gate)))
        ).astype(jnp.bfloat16)
        grad_up_act = (grad_hidden * silu_gate).astype(jnp.bfloat16)
        grad_gate = contract_rows(normed, grad_gate_act)
        grad_up = contract_rows(normed, grad_up_act)
        grad_normed = contract_cols(grad_gate_act, gate_copy) + contract_cols(grad_up_act, up_copy)
        gain_part = jnp.sum(grad_normed * scaled, axis=0)
        square_part = (
            jnp.sum(grad_gate * grad_gate)
            + jnp.sum(grad_up * grad_up)
            + jnp.sum(grad_down * grad_down)
        )
        flag_part = overflow[0, local_step, 0].astype(jnp.float32)
        grad_gain, squares, flagged = lax.psum((gain_part, square_part, flag_part), "tp")
        grad_norm = jnp.sqrt(squares + jnp.sum(grad_gain * grad_gain) + 1e-06)
        factor = jnp.where(flagged < 0.5, limit / jnp.maximum(grad_norm, limit), 0.0)
        gate_master = gate_master - 0.005 * factor * grad_gate
        up_master = up_master - 0.005 * factor * grad_up
        down_master = down_master - 0.005 * factor * grad_down
        gain_master = gain_master - 0.005 * factor * grad_gain
        gate_total = gate_total + factor * grad_gate
        up_total = up_total + factor * grad_up
        down_total = down_total + factor * grad_down
        gain_total = gain_total + factor * grad_gain
    gate_sum, up_sum, down_sum, gain_sum = (
        lax.psum_scatter(gate_total, "client", scatter_dimension=0, tiled=True),
        lax.psum_scatter(up_total, "client", scatter_dimension=0, tiled=True),
        lax.psum_scatter(down_total, "client", scatter_dimension=1, tiled=True),
        lax.psum_scatter(gain_total, "client", scatter_dimension=0, tiled=True),
    )
    clients = lax.axis_size("client")
    return (gate_sum / clients, up_sum / clients, down_sum / clients, gain_sum / clients)


def solution(mesh):
    placed = (
        P("client", None, None),
        P("client", None, None),
        P(),
        P(None, "tp"),
        P(None, "tp"),
        P("tp", None),
        P("client", None, "tp"),
    )
    return jax.shard_map(
        on_device,
        mesh=mesh,
        in_specs=placed,
        out_specs=(P("client", "tp"), P("client", "tp"), P("tp", "client"), P("client")),
        check_vma=False,
    )
```

profile of v0, /device:TPU:0, one launch (start us, length us, event | category | flops | bytes accessed | tf_op | source)
XLA Modules:
  0.0 554.3 jit_solution(13784394405349076077)
XLA Ops:
  8.6 2.3 fusion.44
  10.9 3.0 multiply_convert_fusion.8
  16.8 79.5 %all-reduce.8.cloned.1.call-done = f32[128,2048]{1,0:T(8,128)} async-done(((f32[128,2048]{1,0:T(8,128)}), f32[128,2048]{1,0:T(8,128)}) %all-reduce.8.cloned.1.call-update) | async-done | bytes 1048592 | tf_op jit(solution)/shard_map/psum | solution.py:49
  97.7 3.4 multiply_reduce_fusion.6
  101.1 2.6 multiply_convert_fusion.6
  103.7 3.3 multiply_reduce_fusion.8
  107.9 3.4 multiply_reduce_fusion.7
  114.1 21.6 %all-reduce.3 = (f32[]{:T(128)}, f32[]{:T(128)}, f32[2048]{0:T(1024)S(1)}) all-reduce(f32[]{:T(128)} %bitcast, f32[]{:T(128)S(6)} %add.145, f32[2048]{0:T(1024)S(1)} %fusion.9), channel_id=1, replica_groups=mesh['client'=4,'tp'=8] {'tp'}, use_global_device_ids=true, to_apply=%region_0.0 | all-reduce | flops 2050 | bytes 16400 | tf_op jit(solution)/shard_map/psum | solution.py:68
  138.3 3.7 fusion.2
  143.9 2.1 copy-done.1
  152.3 74.5 %all-reduce.10.cloned.1.call-done = f32[128,2048]{1,0:T(8,128)} async-done(((f32[128,2048]{1,0:T(8,128)}), f32[128,2048]{1,0:T(8,128)}) %all-reduce.10.cloned.1.call-update) | async-done | bytes 1048592 | tf_op jit(solution)/shard_map/psum | solution.py:49
  228.4 3.3 multiply_reduce_fusion.3
  233.4 3.4 multiply_reduce_fusion.5
  236.8 3.3 multiply_reduce_fusion.4
  242.9 21.6 %all-reduce.2 = (f32[]{:T(128)}, f32[]{:T(128)}, f32[2048]{0:T(1024)S(1)}) all-reduce(f32[]{:T(128)} %bitcast.4, f32[]{:T(128)S(6)} %add.153, f32[2048]{0:T(1024)S(1)} %fusion.10), channel_id=1, replica_groups=mesh['client'=4,'tp'=8] {'tp'}, use_global_device_ids=true, to_apply=%region_10.11 | all-reduce | flops 2050 | bytes 16400 | tf_op jit(solution)/shard_map/psum | solution.py:68
  267.2 5.5 %subtract_convert_fusion = bf16[512,2048]{1,0:T(8,128)(2,1)S(1)} fusion(f32[512,2048]{1,0:T(8,128)} %get-tuple-element.37, f32[512,2048]{1,0:T(8,128)} %get-tuple-element.29, bf16[512,2048]{1,0:T(8,128)(2,1)} %param.12, f32[]{:T(128)S(6)} %mul.308, f32[]{:T(128)S(6)} %mul.284), kind=kLoop, calls=%fused_computation.6 | loop fusion | flops 6291456 | bytes 12582920 | tf_op jit(solution)/shard_map/convert_element_type | solution.py:42
  275.6 4.6 subtract_convert_fusion.1
  286.0 74.3 %all-reduce.12.cloned.1.call-done = f32[128,2048]{1,0:T(8,128)} async-done(((f32[128,2048]{1,0:T(8,128)}), f32[128,2048]{1,0:T(8,128)}) %all-reduce.12.cloned.1.call-update) | async-done | bytes 1048592 | tf_op jit(solution)/shard_map/psum | solution.py:49
  361.8 3.3 multiply_reduce_fusion
  366.7 3.4 multiply_reduce_fusion.2
  370.1 3.5 multiply_reduce_fusion.1
  376.3 21.6 %all-reduce.1 = (f32[]{:T(128)}, f32[]{:T(128)}, f32[2048]{0:T(1024)S(1)}) all-reduce(f32[]{:T(128)} %bitcast.6, f32[]{:T(128)S(6)} %add.162, f32[2048]{0:T(1024)S(1)} %fusion.11), channel_id=1, replica_groups=mesh['client'=4,'tp'=8] {'tp'}, use_global_device_ids=true, to_apply=%region_19.20 | all-reduce | flops 2050 | bytes 16400 | tf_op jit(solution)/shard_map/psum | solution.py:68
  400.6 8.5 %multiply_add_fusion = f32[512,2048]{1,0:T(8,128)} fusion(f32[512,2048]{1,0:T(8,128)} %get-tuple-element.45, f32[512,2048]{1,0:T(8,128)} %get-tuple-element.37, f32[512,2048]{1,0:T(8,128)} %get-tuple-element.29, f32[]{:T(128)S(6)} %select_n.12, f32[]{:T(128)S(6)} %select_n.11, f32[]{:T(128)S(6)} %select_n.10), kind=kLoop, calls=%fused_computation | loop fusion | flops 5242880 | bytes 16777228 | tf_op jit(solution)/shard_map/add | solution.py:77
  409.1 9.0 %multiply_add_fusion.1 = f32[2048,512]{1,0:T(8,128)} fusion(f32[2048,512]{1,0:T(8,128)} %get-tuple-element.43, f32[2048,512]{1,0:T(8,128)} %get-tuple-element.35, f32[2048,512]{1,0:T(8,128)} %get-tuple-element.27, f32[]{:T(128)S(6)} %select_n.12, f32[]{:T(128)S(6)} %select_n.11, f32[]{:T(128)S(6)} %select_n.10), kind=kLoop, calls=%fused_computation.1 | loop fusion | flops 5242880 | bytes 16777228 | tf_op jit(solution)/shard_map/add | solution.py:76
  418.2 8.2 %multiply_add_fusion.2 = f32[2048,512]{1,0:T(8,128)} fusion(f32[2048,512]{1,0:T(8,128)} %get-tuple-element.41, f32[2048,512]{1,0:T(8,128)} %get-tuple-element.33, f32[2048,512]{1,0:T(8,128)} %get-tuple-element.25, f32[]{:T(128)S(6)} %select_n.12, f32[]{:T(128)S(6)} %select_n.11, f32[]{:T(128)S(6)} %select_n.10), kind=kLoop, calls=%fused_computation.2 | loop fusion | flops 5242880 | bytes 16777228 | tf_op jit(solution)/shard_map/add | solution.py:75
  428.3 6.4 %all-reduce = f32[2048]{0:T(1024)S(1)} all-reduce(f32[2048]{0:T(1024)S(1)} %multiply_add_fusion.3), channel_id=5, replica_groups=mesh['client'=4,'tp'=8] {'client'}, use_global_device_ids=true, to_apply=%region_31.32.clone | all-reduce | flops 2048 | bytes 16384
  435.5 15.7 %reduce-scatter.8.cloned.1.call-done = f32[512,512]{1,0:T(8,128)} async-done(((f32[512,2048]{1,0:T(8,128)}), f32[512,512]{1,0:T(8,128)}) %reduce-scatter.8.cloned.1.call-update) | async-done | bytes 1048592 | tf_op jit(solution)/shard_map/reduce_scatter | solution.py:82
  451.2 2.3 broadcast_multiply_fusion
  453.5 44.6 %reduce-scatter.6.cloned.1.call-done = f32[512,512]{1,0:T(8,128)} async-done(((f32[2048,512]{1,0:T(8,128)}), f32[512,512]{1,0:T(8,128)}) %reduce-scatter.6.cloned.1.call-update) | async-done | bytes 1048592 | tf_op jit(solution)/shard_map/reduce_scatter | solution.py:81
  498.1 2.3 broadcast_multiply_fusion.1
  500.4 44.8 %reduce-scatter.4.cloned.1.call-done = f32[512,512]{1,0:T(8,128)} async-done(((f32[2048,512]{1,0:T(8,128)}), f32[512,512]{1,0:T(8,128)}) %reduce-scatter.4.cloned.1.call-update) | async-done | bytes 1048592 | tf_op jit(solution)/shard_map/reduce_scatter | solution.py:80
  545.2 2.3 broadcast_multiply_fusion.2
  (112 shorter events, 33.8 us)
Async XLA Ops:
  7.2 6.8 %copy-start.9 = (bf16[512,2048]{1,0:T(8,128)(2,1)S(1)}, bf16[512,2048]{1,0:T(8,128)(2,1)}, u32[]{:S(2)}) copy-start(bf16[512,2048]{1,0:T(8,128)(2,1)} %param.12) | copy-start | bytes 6291460
  7.2 89.1 %all-reduce.8.cloned.1.call-start = ((), (), s32[]{:S(2)}) async-start(), calls=%async_computation.3 | async-start | bytes 2097152 | tf_op jit(solution)/shard_map/psum | solution.py:49
  8.6 102.7 %copy-start.28 = (f32[128]{0:T(128)}, f32[128]{0:T(128)S(1)}, u32[]{:S(2)}) copy-start(f32[128]{0:T(128)S(1)} %add_rsqrt_fusion) | copy-start | bytes 1540
  10.9 4.6 copy-start.31
  10.9 85.4 %copy-start = (bf16[1,128,2048]{2,1,0:T(8,128)(2,1)S(1)}, bf16[1,128,2048]{2,1,0:T(8,128)(2,1)}, u32[]{:S(2)}) copy-start(bf16[1,128,2048]{2,1,0:T(8,128)(2,1)} %param.7) | copy-start | bytes 1572868
  10.9 85.4 %copy-start.22 = (bf16[1,128,2048]{2,1,0:T(8,128)(2,1)S(1)}, bf16[1,128,2048]{2,1,0:T(8,128)(2,1)}, u32[]{:S(2)}) copy-start(bf16[1,128,2048]{2,1,0:T(8,128)(2,1)} %param.8) | copy-start | bytes 1572868
  15.4 211.4 %all-reduce.10.cloned.1.call-start = ((), (), s32[]{:S(2)}) async-start(), calls=%async_computation.4 | async-start | bytes 2097152 | tf_op jit(solution)/shard_map/psum | solution.py:49
  97.7 6.0 %copy-start.23 = (f32[2048]{0:T(1024)S(1)}, f32[2048]{0:T(1024)}, u32[]{:S(2)}) copy-start(f32[2048]{0:T(1024)} %param.9) | copy-start | bytes 24580
  101.1 6.0 %copy-start.6 = (bf16[2048,512]{1,0:T(8,128)(2,1)S(1)}, bf16[2048,512]{1,0:T(8,128)(2,1)}, u32[]{:S(2)}) copy-start(bf16[2048,512]{1,0:T(8,128)(2,1)} %param.10) | copy-start | bytes 6291460
  107.1 4.2 copy-start.10
  135.7 6.4 %copy-start.24 = (f32[2048]{0:T(1024)}, f32[2048]{0:T(1024)S(1)}, u32[]{:S(2)}) copy-start(f32[2048]{0:T(1024)S(1)} %get-tuple-element.12) | copy-start | bytes 24580
  138.3 4.7 copy-start.11
  142.1 7.9 %copy-start.20 = (bf16[512,2048]{1,0:T(8,128)(2,1)}, bf16[512,2048]{1,0:T(8,128)(2,1)S(1)}, u32[]{:S(2)}) copy-start(bf16[512,2048]{1,0:T(8,128)(2,1)S(1)} %fusion.2) | copy-start | bytes 6291460
  143.9 4.9 copy-start.18
  151.5 208.8 %all-reduce.12.cloned.1.call-start = ((), (), s32[]{:S(2)}) async-start(), calls=%async_computation.5 | async-start | bytes 2097152 | tf_op jit(solution)/shard_map/psum | solution.py:49
  226.8 4.9 copy-start.21
  226.8 4.9 copy-start.34
  228.4 4.2 copy-start.13
  233.4 6.7 %copy-start.19 = (bf16[2048,512]{1,0:T(8,128)(2,1)S(1)}, bf16[2048,512]{1,0:T(8,128)(2,1)}, u32[]{:S(2)}) copy-start(bf16[2048,512]{1,0:T(8,128)(2,1)} %copy-done.18) | copy-start | bytes 6291460
  264.5 8.2 %copy-start.26 = (f32[2048]{0:T(1024)}, f32[2048]{0:T(1024)S(1)}, u32[]{:S(2)}) copy-start(f32[2048]{0:T(1024)S(1)} %get-tuple-element.9) | copy-start | bytes 24580
  267.2 5.6 %copy-start.2 = (f32[2048,512]{1,0:T(8,128)S(1)}, f32[2048,512]{1,0:T(8,128)}, u32[]{:S(2)}) copy-start(f32[2048,512]{1,0:T(8,128)} %get-tuple-element.25) | copy-start | bytes 12582916
  267.2 6.5 %copy-start.4 = (f32[2048,512]{1,0:T(8,128)S(1)}, f32[2048,512]{1,0:T(8,128)}, u32[]{:S(2)}) copy-start(f32[2048,512]{1,0:T(8,128)} %get-tuple-element.27) | copy-start | bytes 12582916
  267.2 8.5 %copy-start.5 = (f32[2048,512]{1,0:T(8,128)S(1)}, f32[2048,512]{1,0:T(8,128)}, u32[]{:S(2)}) copy-start(f32[2048,512]{1,0:T(8,128)} %get-tuple-element.33) | copy-start | bytes 12582916
  272.7 10.7 %copy-start.16 = (bf16[512,2048]{1,0:T(8,128)(2,1)}, bf16[512,2048]{1,0:T(8,128)(2,1)S(1)}, u32[]{:S(2)}) copy-start(bf16[512,2048]{1,0:T(8,128)(2,1)S(1)} %subtract_convert_fusion) | copy-start | bytes 6291460
  275.6 5.9 %copy-start.30 = (f32[128]{0:T(128)S(1)}, f32[128]{0:T(128)}, u32[]{:S(2)}) copy-start(f32[128]{0:T(128)} %copy-done.28) | copy-start | bytes 1540
  284.9 80.1 %copy-start.17 = (bf16[512,2048]{1,0:T(8,128)(2,1)S(1)}, bf16[512,2048]{1,0:T(8,128)(2,1)}, u32[]{:S(2)}) copy-start(bf16[512,2048]{1,0:T(8,128)(2,1)} %copy-done.16) | copy-start | bytes 6291460
  284.9 166.3 %reduce-scatter.8.cloned.1.call-start = ((), (), s32[]{:S(2)}) async-start(), calls=%async_computation.8 | async-start | bytes 5242880 | tf_op jit(solution)/shard_map/reduce_scatter | solution.py:82
  360.3 4.8 copy-start.33
  361.7 4.2 copy-start.8
  366.7 6.9 %copy-start.15 = (bf16[2048,512]{1,0:T(8,128)(2,1)S(1)}, bf16[2048,512]{1,0:T(8,128)(2,1)}, u32[]{:S(2)}) copy-start(bf16[2048,512]{1,0:T(8,128)(2,1)} %copy-done.14) | copy-start | bytes 6291460
  409.0 89.1 %reduce-scatter.6.cloned.1.call-start = ((), (), s32[]{:S(2)}) async-start(), calls=%async_computation.7 | async-start | bytes 5242880 | tf_op jit(solution)/shard_map/reduce_scatter | solution.py:81
  418.2 127.1 %reduce-scatter.4.cloned.1.call-start = ((), (), s32[]{:S(2)}) async-start(), calls=%async_computation.6 | async-start | bytes 5242880 | tf_op jit(solution)/shard_map/reduce_scatter | solution.py:80
  (9 other events, 18.4 us)
Sparse Core Ops, SparseCore 0:
  15.5 80.7 all-reduce.7
  151.6 75.2 all-reduce.9
  285.1 75.1 all-reduce.11
  409.2 41.9 reduce-scatter.7
  453.6 44.4 reduce-scatter.5
  500.7 44.5 reduce-scatter.3
where the time goes:
time: 555 us; the launch traced here: 554 us
  waiting for transfers between devices  334 us (60%)
  blocking collectives  71.2 us (13%)
  other arithmetic  56.4 us (10%)
  matrix products  52.5 us (9%)
  between operations  29.2 us (5%)
  local copies, waits for them, and re-layouts  10.8 us (2%)
    psum x3, waiting for transfers between devices, on_device(): summed = lax.psum(partial_value, 'tp')  228 us
    psum x3, blocking collectives, on_device(): lax.psum((gain_part, square_part, flag_part), 'tp')  64.8 us
    reduce_scatter x1, waiting for transfers between devices, on_device(): lax.psum_scatter(gate_total, 'client', scatter_dimension=0, tiled=True)  44.8 us
    reduce_scatter x1, waiting for transfers between devices, on_device(): lax.psum_scatter(up_total, 'client', scatter_dimension=0, tiled=True)  44.6 us
    dot_general x9, matrix products, contract_rows(): lax.dot_general(left, right, (((0,), (0,)), ((), ())), preferred_element_...  30.2 us
    reduce_scatter x1, waiting for transfers between devices, on_device(): lax.psum_scatter(down_total, 'client', scatter_dimension=1, tiled=True)  15.7 us
  transfers between devices with their start and end apart: 6, of which 6 were waited for; matrix products, arithmetic and copies ran while one was open for 4% of the time, Pallas kernels for 0%

commit v1 on v0

v1 whole, which is shorter than its diff:
```python
import functools
import math

import jax
import jax.numpy as jnp
from jax import lax
from jax.experimental import pallas as pl
from jax.experimental.pallas import tpu as pltpu
from jax.sharding import PartitionSpec as P

LR = 0.005
F32 = jnp.float32
BF16 = jnp.bfloat16
MESH = pl.DeviceIdType.MESH


def mm(left, right):
    return lax.dot_general(left, right, (((1,), (0,)), ((), ())), preferred_element_type=F32)


def mm_nt(left, right):
    return lax.dot_general(left, right, (((1,), (1,)), ((), ())), preferred_element_type=F32)


def mm_tn(left, right):
    return lax.dot_general(left, right, (((0,), (0,)), ((), ())), preferred_element_type=F32)


def sum_all(value):
    return jnp.sum(jnp.sum(value, axis=0, keepdims=True), axis=1, keepdims=True)


def kernel(
    n_tp, n_cl, steps, limit,
    x_ref, t_ref, gain_ref, wg_ref, wu_ref, wd_ref, flag_ref,
    og_ref, ou_ref, od_ref, ogain_ref,
    scaled, gain, n_buf, o_buf, part, rs_buf, sm_buf, n_cli, o_cli, h_cli, g_cli, fin,
    ga, ua, sg, gh, hh, oo, coef,
    rs_s, rs_r, ag_s, ag_r, sm_s, sm_r, cn_s, cn_r, ch_s, ch_r, co_s, co_r, cg_s, cg_r, fi_s, fi_r,
):
    tp = lax.axis_index("tp")
    cl = lax.axis_index("client")
    tok, width = x_ref.shape
    dt = width // n_tp
    ds = width // n_cl
    q = ds // dt

    def tp_peer(k):
        return lax.rem(tp + k, n_tp)

    def cl_peer(k):
        return lax.rem(cl + k, n_cl)

    barrier = pltpu.get_barrier_semaphore()

    @pl.loop(1, n_tp)
    def _(k):
        pl.semaphore_signal(barrier, inc=1, device_id={"tp": tp_peer(k)}, device_id_type=MESH)

    @pl.loop(1, n_cl)
    def _(k):
        pl.semaphore_signal(barrier, inc=1, device_id={"client": cl_peer(k)}, device_id_type=MESH)

    def lanes(p):
        return pl.ds(pl.multiple_of(p * dt, dt), dt)

    def slice_of(c):
        return pl.ds(pl.multiple_of(c * ds, ds), ds)

    def tp_copy(src, dst, send, recv, k):
        return pltpu.make_async_remote_copy(
            src_ref=src, dst_ref=dst, send_sem=send, recv_sem=recv,
            device_id={"tp": tp_peer(k)}, device_id_type=MESH)

    def cl_copy(src, dst, send, recv, k):
        return pltpu.make_async_remote_copy(
            src_ref=src, dst_ref=dst, send_sem=send, recv_sem=recv,
            device_id={"client": cl_peer(k)}, device_id_type=MESH)

    def rs_copy(s, k):
        return tp_copy(part.at[tp_peer(k)], rs_buf.at[s, k - 1], rs_s.at[k - 1], rs_r.at[s, k - 1], k)

    def ag_copy(s, k):
        own = o_buf.at[s, :, lanes(tp)]
        return tp_copy(own, own, ag_s.at[k - 1], ag_r.at[s, k - 1], k)

    def ag_arrival(s, k):
        theirs = o_buf.at[s, :, lanes(tp_peer(n_tp - k))]
        return tp_copy(theirs, theirs, ag_s.at[k - 1], ag_r.at[s, k - 1], k)

    def sm_copy(s, k):
        own = sm_buf.at[s, tp]
        return tp_copy(own, own, sm_s.at[k - 1], sm_r.at[s, k - 1], k)

    def sm_arrival(s, k):
        theirs = sm_buf.at[s, tp_peer(n_tp - k)]
        return tp_copy(theirs, theirs, sm_s.at[k - 1], sm_r.at[s, k - 1], k)

    def from_cl(k):
        return cl_peer(n_cl - k)

    def cn_copy(s, k, c):
        return cl_copy(n_buf.at[s, :, slice_of(cl_peer(k))], n_cli.at[s, c], cn_s.at[s, k - 1], cn_r.at[s, k - 1], k)

    def co_copy(s, k, c):
        return cl_copy(o_buf.at[s, :, slice_of(cl_peer(k))], o_cli.at[s, c], co_s.at[s, k - 1], co_r.at[s, k - 1], k)

    def ch_copy(s, k, c):
        return cl_copy(h_cli.at[s, c], h_cli.at[s, c], ch_s.at[s, k - 1], ch_r.at[s, k - 1], k)

    def cg_copy(s, k, c):
        return cl_copy(g_cli.at[:, s, c], g_cli.at[:, s, c], cg_s.at[s, k - 1], cg_r.at[s, k - 1], k)

    def fi_copy(k, c):
        return cl_copy(fin.at[c], fin.at[c], fi_s.at[k - 1], fi_r.at[k - 1], k)

    x = x_ref[...].astype(F32)
    scaled[...] = x * lax.rsqrt(jnp.mean(x * x, axis=-1, keepdims=True) + 1e-05)
    gain[...] = gain_ref[...]
    for p in range(n_tp):
        fin[cl, steps + p] = jnp.zeros((1, dt), F32)

    def step(s, carry):
        for p in range(n_tp):
            at = slice(p * dt, (p + 1) * dt)
            n_buf[s, :, at] = (scaled[:, at] * gain[p]).astype(BF16)

        @pl.when(s == 0)
        def _():
            pl.semaphore_wait(barrier, n_tp - 1 + n_cl - 1)

        @pl.loop(1, n_cl)
        def _(k):
            cn_copy(s, k, cl).start()

        normed = n_buf[s]
        ga[...] = mm(normed, wg_ref[...])
        ua[...] = mm(normed, wu_ref[...])

        @pl.loop(0, s)
        def _(j):
            p = (mm_nt(n_buf[s], n_buf[j]) * coef[j]).astype(BF16)
            ga[...] += mm(p, g_cli[0, j, cl])
            ua[...] += mm(p, g_cli[1, j, cl])

        gate = ga[...]
        sig = jax.nn.sigmoid(gate)
        silu = gate * sig
        sg[...] = sig
        h_cli[s, cl] = (silu * ua[...]).astype(BF16)

        @pl.loop(0, s + 1)
        def _(j):
            hh[j] = mm_nt(h_cli[s, cl], h_cli[j, cl])

        def out_chunk(p):
            first = mm(h_cli[s, cl], wd_ref[:, lanes(p)])

            def more(j, acc):
                return acc + mm((hh[j] * coef[j]).astype(BF16), o_buf[j, :, lanes(p)])

            return lax.fori_loop(0, s, more, first)

        @pl.loop(1, n_tp)
        def _(k):
            part[tp_peer(k)] = out_chunk(tp_peer(k)).astype(BF16)
            rs_copy(s, k).start()

        summed = out_chunk(tp)

        @pl.loop(1, n_cl)
        def _(k):
            ch_copy(s, k, cl).start()

        summed = summed + (x_ref[:, lanes(tp)].astype(F32) - t_ref[:, lanes(tp)].astype(F32))
        for k in range(1, n_tp):
            rs_copy(s, k).wait_recv()
            summed = summed + rs_buf[s, k - 1].astype(F32)
        o_buf[s, :, lanes(tp)] = summed.astype(BF16)

        @pl.loop(1, n_tp)
        def _(k):
            ag_copy(s, k).start()

        gh[...] = mm_nt(o_buf[s, :, lanes(tp)], wd_ref[:, lanes(tp)])
        for k in range(1, n_tp):
            ag_arrival(s, k).wait_recv()
            at = lanes(tp_peer(n_tp - k))
            gh[...] += mm_nt(o_buf[s, :, at], wd_ref[:, at])

        @pl.loop(1, n_cl)
        def _(k):
            co_copy(s, k, cl).start()

        @pl.loop(0, s)
        def _(j):
            p = (mm_nt(o_buf[s], o_buf[j]) * coef[j]).astype(BF16)
            gh[...] += mm(p, h_cli[j, cl])

        oo[...] = mm_nt(o_buf[s], o_buf[s])
        sig = sg[...]
        gate = ga[...]
        grad_hidden = gh[...]
        gg = (grad_hidden * ua[...] * (sig * (1.0 + gate * (1.0 - sig)))).astype(BF16)
        gu = (grad_hidden * (gate * sig)).astype(BF16)
        g_cli[0, s, cl] = gg
        g_cli[1, s, cl] = gu

        @pl.loop(1, n_cl)
        def _(k):
            cg_copy(s, k, cl).start()

        squares = sum_all(mm_nt(n_buf[s], n_buf[s]) * (mm_nt(gg, gg) + mm_nt(gu, gu)) + hh[s] * oo[...])
        sm_buf[s, tp, n_tp] = jnp.broadcast_to(squares, (1, dt))
        sm_buf[s, tp, n_tp + 1] = flag_ref[s]

        @pl.loop(0, s)
        def _(j):
            oo_j = mm_nt(g_cli[0, s, cl], g_cli[0, j, cl]) + mm_nt(g_cli[1, s, cl], g_cli[1, j, cl])
            hh[j] = oo_j * coef[j]

        @pl.loop(0, n_tp)
        def _(p):
            rows = pl.ds(pl.multiple_of(p * dt, dt), dt)
            first = mm_nt(g_cli[0, s, cl], wg_ref[rows, :]) + mm_nt(g_cli[1, s, cl], wu_ref[rows, :])

            def more(j, acc):
                return acc + mm(hh[j].astype(BF16), n_buf[j, :, lanes(p)])

            grad_normed = lax.fori_loop(0, s, more, first)
            sm_buf[s, tp, p] = jnp.sum(grad_normed * scaled[:, lanes(p)], axis=0, keepdims=True)

        @pl.loop(1, n_tp)
        def _(k):
            sm_copy(s, k).start()

        @pl.loop(1, n_tp)
        def _(k):
            rs_copy(s, k).wait_send()
            ag_copy(s, k).wait_send()

        @pl.loop(1, n_tp)
        def _(k):
            sm_arrival(s, k).wait_recv()

        total = sm_buf[s, 0]
        for t in range(1, n_tp):
            total = total + sm_buf[s, t]
        gain_grad = total[:n_tp]
        gain_square = jnp.sum(jnp.sum(gain_grad * gain_grad, axis=0), axis=1, keepdims=True)
        norm = jnp.sqrt(jnp.maximum(total[n_tp], 0.0) + gain_square + 1e-06)
        factor = jnp.where(total[n_tp + 1] < 0.5, limit / jnp.maximum(norm, limit), 0.0)
        fin[cl, s] = factor
        coef[s] = jnp.broadcast_to(factor[:, :tok] * (-LR), (1, tok))
        for p in range(n_tp):
            change = factor * gain_grad[p]
            gain[p] = gain[p] - LR * change
            fin[cl, steps + p] = fin[cl, steps + p] + change

        @pl.loop(1, n_tp)
        def _(k):
            sm_copy(s, k).wait_send()

        n_cli[s, cl] = n_buf[s, :, slice_of(cl)]
        o_cli[s, cl] = o_buf[s, :, slice_of(cl)]
        return carry

    lax.fori_loop(0, steps, step, 0)

    @pl.loop(1, n_cl)
    def _(k):
        fi_copy(k, cl).start()

    @pl.loop(0, steps)
    def _(s):
        @pl.loop(1, n_cl)
        def _(k):
            c = from_cl(k)
            cn_copy(s, k, c).wait_recv()
            ch_copy(s, k, c).wait_recv()
            co_copy(s, k, c).wait_recv()
            cg_copy(s, k, c).wait_recv()
            cn_copy(s, k, cl).wait_send()
            ch_copy(s, k, cl).wait_send()
            co_copy(s, k, cl).wait_send()
            cg_copy(s, k, cl).wait_send()

    @pl.loop(1, n_cl)
    def _(k):
        fi_copy(k, from_cl(k)).wait_recv()
        fi_copy(k, cl).wait_send()

    for i in range(q):
        acc = fin[0, steps + cl * q + i]
        for c in range(1, n_cl):
            acc = acc + fin[c, steps + cl * q + i]
        ogain_ref[i] = acc * (1.0 / n_cl)

    @pl.loop(0, n_cl)
    def _(c):
        @pl.loop(0, steps)
        def _(s):
            f = fin[c, s][:, :1] * (1.0 / n_cl)
            n_cli[s, c] = (n_cli[s, c].astype(F32) * f).astype(BF16)
            o_cli[s, c] = (o_cli[s, c].astype(F32) * f).astype(BF16)

    rows = steps * n_cl * tok
    ff = wg_ref.shape[1]
    n_all = n_cli[...].reshape(rows, ds)
    og_ref[...] = mm_tn(n_all, g_cli[0].reshape(rows, ff))
    ou_ref[...] = mm_tn(n_all, g_cli[1].reshape(rows, ff))
    od_ref[...] = mm_tn(h_cli[...].reshape(rows, ff), o_cli[...].reshape(rows, ds))


def on_device(n_tp, n_cl, inputs, targets, norm_gain, gate_weight, up_weight, down_weight, overflow):
    tok, width = inputs.shape[1:]
    ff = gate_weight.shape[1]
    steps = overflow.shape[1]
    dt = width // n_tp
    ds = width // n_cl
    limit = 0.5 * math.sqrt(3.0 * width * ff * n_tp)
    flags = jnp.broadcast_to(overflow.astype(F32).reshape(steps, 1, 1), (steps, 1, dt))
    gain = norm_gain.reshape(n_tp, 1, dt)
    dma = pltpu.SemaphoreType.DMA
    vmem = pl.BlockSpec(memory_space=pltpu.VMEM)
    gate, up, down, gain_out = pl.pallas_call(
        functools.partial(kernel, n_tp, n_cl, steps, limit),
        out_shape=(
            jax.ShapeDtypeStruct((ds, ff), F32),
            jax.ShapeDtypeStruct((ds, ff), F32),
            jax.ShapeDtypeStruct((ff, ds), F32),
            jax.ShapeDtypeStruct((ds // dt, 1, dt), F32),
        ),
        in_specs=[vmem] * 7,
        out_specs=(vmem,) * 4,
        scratch_shapes=[
            pltpu.VMEM((tok, width), F32),
            pltpu.VMEM((n_tp, 1, dt), F32),
            pltpu.VMEM((steps, tok, width), BF16),
            pltpu.VMEM((steps, tok, width), BF16),
            pltpu.VMEM((n_tp, tok, dt), BF16),
            pltpu.VMEM((steps, n_tp - 1, tok, dt), BF16),
            pltpu.VMEM((steps, n_tp, n_tp + 2, 1, dt), F32),
            pltpu.VMEM((steps, n_cl, tok, ds), BF16),
            pltpu.VMEM((steps, n_cl, tok, ds), BF16),
            pltpu.VMEM((steps, n_cl, tok, ff), BF16),
            pltpu.VMEM((2, steps, n_cl, tok, ff), BF16),
            pltpu.VMEM((n_cl, steps + n_tp, 1, dt), F32),
            pltpu.VMEM((tok, ff), F32),
            pltpu.VMEM((tok, ff), F32),
            pltpu.VMEM((tok, ff), F32),
            pltpu.VMEM((tok, ff), F32),
            pltpu.VMEM((steps, tok, tok), F32),
            pltpu.VMEM((tok, tok), F32),
            pltpu.VMEM((steps, 1, tok), F32),
            dma((n_tp - 1,)), dma((steps, n_tp - 1)),
            dma((n_tp - 1,)), dma((steps, n_tp - 1)),
            dma((n_tp - 1,)), dma((steps, n_tp - 1)),
            dma((steps, n_cl - 1)), dma((steps, n_cl - 1)),
            dma((steps, n_cl - 1)), dma((steps, n_cl - 1)),
            dma((steps, n_cl - 1)), dma((steps, n_cl - 1)),
            dma((steps, n_cl - 1)), dma((steps, n_cl - 1)),
            dma((n_cl - 1,)), dma((n_cl - 1,)),
        ],
        compiler_params=pltpu.CompilerParams(
            collective_id=0, has_side_effects=True, vmem_limit_bytes=48 * 1024 * 1024
        ),
        name="fedavg_round",
    )(inputs[0], targets[0], gain, gate_weight, up_weight, down_weight, flags)
    return gate, up, down, gain_out.reshape(ds)


def solution(mesh):
    placed = (
        P("client", None, None),
        P("client", None, None),
        P(),
        P(None, "tp"),
        P(None, "tp"),
        P("tp", None),
        P("client", None, "tp"),
    )
    return jax.shard_map(
        functools.partial(on_device, mesh.shape["tp"], mesh.shape["client"]),
        mesh=mesh,
        in_specs=placed,
        out_specs=(P("client", "tp"), P("client", "tp"), P("tp", "client"), P("client")),
        check_vma=False,
    )
```

time: 555 us -> 146 us (0.26)
  waiting for transfers between devices: 334 us -> 0 us
  Pallas kernels: 0 us -> 137 us
  blocking collectives: 71.2 us -> 0 us
  other arithmetic: 56.4 us -> 0.66 us
  matrix products: 52.5 us -> 0 us
  between operations: 29.2 us -> 0.64 us
    psum x3 -> x0, waiting for transfers between devices: 228 us -> none  [on_device(): summed = lax.psum(partial_value, 'tp')]
    pallas_call x0 -> x1, Pallas kernels: none -> 137 us  [on_device(): pl.pallas_call(functools.partial(kernel, n_tp, n_cl, steps, limit), out_s...]
    reduce_scatter x3 -> x0, waiting for transfers between devices: 105 us -> none  [the longest x1 44.8 us: on_device(): lax.psum_scatter(gate_total, 'client', scatter_dimension=0, tiled=True)]
    psum x3 -> x0, blocking collectives: 64.8 us -> none  [on_device(): lax.psum((gain_part, square_part, flag_part), 'tp')]
    dot_general x27 -> x0, matrix products: 52.5 us -> none  [the longest x9 30.2 us: contract_rows(): lax.dot_general(left, right, (((0,), (0,)), ((), ())), preferred_element_...]
    add x4 -> x0, other arithmetic: 25.7 us -> none  [the longest x1 9.03 us: on_device(): up_total = up_total + factor * grad_up]
    convert_element_type x8 -> x0, other arithmetic: 19.9 us -> none  [the longest x2 9.26 us: on_device(): down_copy = down_master.astype(jnp.bfloat16)]
    div x4 -> x0, other arithmetic: 7.53 us -> none  [the longest x1 2.29 us: on_device(): up_sum / clients]
  transfers between devices with their start and end apart: 6 -> 0, of which waited for: 6 -> 0; matrix products, arithmetic and copies ran while one was open for 4% -> 0% of each run, Pallas kernels for 0% -> 0%
where the time goes in v1:
time: 146 us; the launch traced here: 145 us
  Pallas kernels  137 us (94%)
  local copies, waits for them, and re-layouts  6.34 us (4%)
    pallas_call x1, Pallas kernels, on_device(): pl.pallas_call(functools.partial(kernel, n_tp, n_cl, steps, limit), out_s...  137 us
    unnamed x10, local copies, waits for them, and re-layouts  6.27 us

profile of v1, /device:TPU:0, one launch (start us, length us, event | category | flops | bytes accessed | tf_op | source)
XLA Modules:
  0.0 144.5 jit_solution(6418309684915110148)
XLA Ops:
  0.6 0.7 convert_bitcast_fusion
  1.3 0.1 broadcast_in_dim.8.flag_ref
  1.4 0.0 copy-start
  1.4 1.0 copy-done
  2.4 0.0 copy-start.1
  2.4 1.0 copy-done.1
  3.4 0.0 copy-start.2
  3.5 0.7 copy-done.2
  4.1 136.9 %fedavg_round.1 = (f32[512,512]{1,0:T(8,128)S(1)}, f32[512,512]{1,0:T(8,128)S(1)}, f32[512,512]{1,0:T(8,128)S(1)}, f32[2,1,256]{2,1,0:T(1,128)S(1)}) custom-call(bf16[128,2048]{1,0:T(8,128)(2,1)S(1)} %bitcast.6, bf16[128,2048]{1,0:T(8,128)(2,1)S(1)} %bitcast.7, f32[8,1,256]{2,1,0:T(1,128)S(1)} %bitcast.8, bf16[2048,512]{1,0:T(8,128)(2,1)} %wg_ref.1, ...), custom_call_target="tpu_custom_call" | custom-call | tf_op jit(solution)/shard_map/fedavg_round/pallas_call | solution.py:326
  141.0 1.0 copy.15
  142.0 1.0 copy.16
  143.0 1.0 copy.17
  143.9 0.6 copy.18
Async XLA Ops:
  1.4 1.0 copy-start
  2.4 1.0 copy-start.1
  3.4 0.7 copy-start.2

commit v2 on v1

--- a/solution.py
+++ b/solution.py
@@ -34,9 +34,10 @@
     n_tp, n_cl, steps, limit,
     x_ref, t_ref, gain_ref, wg_ref, wu_ref, wd_ref, flag_ref,
     og_ref, ou_ref, od_ref, ogain_ref,
-    scaled, gain, n_buf, o_buf, part, rs_buf, sm_buf, n_cli, o_cli, h_cli, g_cli, fin,
+    scaled, gain, n_buf, o_buf, part, pair_buf, line_buf, sm_buf, n_cli, o_cli, h_cli, g_cli, fin,
     ga, ua, sg, gh, hh, oo, coef,
-    rs_s, rs_r, ag_s, ag_r, sm_s, sm_r, cn_s, cn_r, ch_s, ch_r, co_s, co_r, cg_s, cg_r, fi_s, fi_r,
+    rp_s, rp_r, rl_s, rl_r, ap_s, ap_r, al_s, al_r, sm_s, sm_r,
+    cn_s, cn_r, ch_s, ch_r, co_s, co_r, cg_s, cg_r, fi_s, fi_r,
 ):
     tp = lax.axis_index("tp")
     cl = lax.axis_index("client")
@@ -77,16 +78,39 @@
             src_ref=src, dst_ref=dst, send_sem=send, recv_sem=recv,
             device_id={"client": cl_peer(k)}, device_id_type=MESH)
 
-    def rs_copy(s, k):
-        return tp_copy(part.at[tp_peer(k)], rs_buf.at[s, k - 1], rs_s.at[k - 1], rs_r.at[s, k - 1], k)
-
-    def ag_copy(s, k):
-        own = o_buf.at[s, :, lanes(tp)]
-        return tp_copy(own, own, ag_s.at[k - 1], ag_r.at[s, k - 1], k)
-
-    def ag_arrival(s, k):
-        theirs = o_buf.at[s, :, lanes(tp_peer(n_tp - k))]
-        return tp_copy(theirs, theirs, ag_s.at[k - 1], ag_r.at[s, k - 1], k)
+    line = n_tp // 2
+    side = lax.rem(tp, 2)
+    spot = lax.div(tp, 2)
+    pair = tp + 1 - 2 * side
+    sibling = cl + 1 - 2 * lax.rem(cl, 2)
+    pairs = n_cl // 2
+
+    def on_line(k):
+        return lax.rem(spot + k, line) * 2
+
+    def to_tp(src, dst, send, recv, peer):
+        return pltpu.make_async_remote_copy(
+            src_ref=src, dst_ref=dst, send_sem=send, recv_sem=recv,
+            device_id={"tp": peer}, device_id_type=MESH)
+
+    def to_cl(src, dst, send, recv, peer):
+        return pltpu.make_async_remote_copy(
+            src_ref=src, dst_ref=dst, send_sem=send, recv_sem=recv,
+            device_id={"client": peer}, device_id_type=MESH)
+
+    def rp_copy(s, k):
+        return to_tp(part.at[0, k], pair_buf.at[s, k], rp_s.at[k], rp_r.at[s, k], pair)
+
+    def rl_copy(s, k):
+        return to_tp(part.at[1, k], line_buf.at[s, k - 1], rl_s.at[k - 1], rl_r.at[s, k - 1], on_line(k) + side)
+
+    def al_copy(s, k, p):
+        block = o_buf.at[s, :, lanes(p)]
+        return to_tp(block, block, al_s.at[k - 1], al_r.at[s, k - 1], on_line(k) + side)
+
+    def ap_copy(s, k, p):
+        block = o_buf.at[s, :, lanes(p)]
+        return to_tp(block, block, ap_s.at[k], ap_r.at[s, k], pair)
 
     def sm_copy(s, k):
         own = sm_buf.at[s, tp]
@@ -105,20 +129,63 @@
     def co_copy(s, k, c):
         return cl_copy(o_buf.at[s, :, slice_of(cl_peer(k))], o_cli.at[s, c], co_s.at[s, k - 1], co_r.at[s, k - 1], k)
 
-    def ch_copy(s, k, c):
-        return cl_copy(h_cli.at[s, c], h_cli.at[s, c], ch_s.at[s, k - 1], ch_r.at[s, k - 1], k)
-
-    def cg_copy(s, k, c):
-        return cl_copy(g_cli.at[:, s, c], g_cli.at[:, s, c], cg_s.at[s, k - 1], cg_r.at[s, k - 1], k)
-
-    def fi_copy(k, c):
-        return cl_copy(fin.at[c], fin.at[c], fi_s.at[k - 1], fi_r.at[k - 1], k)
+    def far(m):
+        return lax.rem(lax.div(cl, 2) + m, pairs) * 2 + lax.rem(cl, 2)
+
+    def ch_far(s, m, c):
+        block = h_cli.at[s, c]
+        return to_cl(block, block, ch_s.at[s, m - 1], ch_r.at[s, m - 1], far(m))
+
+    def ch_near(s, m, c):
+        block = h_cli.at[s, c]
+        return to_cl(block, block, ch_s.at[s, pairs - 1 + m], ch_r.at[s, pairs - 1 + m], sibling)
+
+    def cg_far(s, m, c):
+        block = g_cli.at[:, s, c]
+        return to_cl(block, block, cg_s.at[s, m - 1], cg_r.at[s, m - 1], far(m))
+
+    def cg_near(s, m, c):
+        block = g_cli.at[:, s, c]
+        return to_cl(block, block, cg_s.at[s, pairs - 1 + m], cg_r.at[s, pairs - 1 + m], sibling)
+
+    def fi_copy(s, k, c):
+        return cl_copy(fin.at[s, c], fin.at[s, c], fi_s.at[s, k - 1], fi_r.at[s, k - 1], k)
+
+    def forward(s):
+        for m in range(1, pairs):
+            source = far(pairs - m)
+            ch_far(s, m, source).wait_recv()
+            ch_near(s, m, source).start()
+            cg_far(s, m, source).wait_recv()
+            cg_near(s, m, source).start()
+
+    def add_out(s):
+        for k in range(1, n_cl):
+            c = from_cl(k)
+            fi_copy(s, k, c).wait_recv()
+            cn_copy(s, k, c).wait_recv()
+            co_copy(s, k, c).wait_recv()
+        for m in range(pairs):
+            c = sibling if m == 0 else far(pairs - m) + 1 - 2 * lax.rem(cl, 2)
+            ch_near(s, m, c).wait_recv()
+            cg_near(s, m, c).wait_recv()
+        for c in range(n_cl):
+            f = fin[s, c, n_tp][:, :1] * (1.0 / n_cl)
+            n_cli[s, c] = (n_cli[s, c].astype(F32) * f).astype(BF16)
+            o_cli[s, c] = (o_cli[s, c].astype(F32) * f).astype(BF16)
+        rows = n_cl * tok
+        ff = wg_ref.shape[1]
+        n_all = n_cli[s].reshape(rows, ds)
+        og_ref[...] += mm_tn(n_all, g_cli[0, s].reshape(rows, ff))
+        ou_ref[...] += mm_tn(n_all, g_cli[1, s].reshape(rows, ff))
+        od_ref[...] += mm_tn(h_cli[s].reshape(rows, ff), o_cli[s].reshape(rows, ds))
 
     x = x_ref[...].astype(F32)
     scaled[...] = x * lax.rsqrt(jnp.mean(x * x, axis=-1, keepdims=True) + 1e-05)
     gain[...] = gain_ref[...]
-    for p in range(n_tp):
-        fin[cl, steps + p] = jnp.zeros((1, dt), F32)
+    og_ref[...] = jnp.zeros_like(og_ref)
+    ou_ref[...] = jnp.zeros_like(ou_ref)
+    od_ref[...] = jnp.zeros_like(od_ref)
 
     def step(s, carry):
         for p in range(n_tp):
@@ -161,31 +228,52 @@
 
             return lax.fori_loop(0, s, more, first)
 
-        @pl.loop(1, n_tp)
-        def _(k):
-            part[tp_peer(k)] = out_chunk(tp_peer(k)).astype(BF16)
-            rs_copy(s, k).start()
-
-        summed = out_chunk(tp)
-
-        @pl.loop(1, n_cl)
-        def _(k):
-            ch_copy(s, k, cl).start()
+        order = list(range(1, line)) + [0]
+        for k in order:
+            part[0, k] = out_chunk(on_line(k) + 1 - side).astype(BF16)
+            rp_copy(s, k).start()
+        for k in order:
+            summed = out_chunk(on_line(k) + side)
+            rp_copy(s, k).wait_recv()
+            summed = summed + pair_buf[s, k].astype(F32)
+            if k > 0:
+                part[1, k] = summed.astype(BF16)
+                rl_copy(s, k).start()
 
         summed = summed + (x_ref[:, lanes(tp)].astype(F32) - t_ref[:, lanes(tp)].astype(F32))
-        for k in range(1, n_tp):
-            rs_copy(s, k).wait_recv()
-            summed = summed + rs_buf[s, k - 1].astype(F32)
+        ch_near(s, 0, cl).start()
+        for m in range(1, pairs):
+            ch_far(s, m, cl).start()
+
+        @pl.when(s > 0)
+        def _():
+            forward(s - 1)
+
+        for k in range(1, line):
+            rl_copy(s, k).wait_recv()
+            summed = summed + line_buf[s, k - 1].astype(F32)
         o_buf[s, :, lanes(tp)] = summed.astype(BF16)
 
-        @pl.loop(1, n_tp)
-        def _(k):
-            ag_copy(s, k).start()
+        ap_copy(s, 0, tp).start()
+        for k in range(1, line):
+            al_copy(s, k, tp).start()
 
         gh[...] = mm_nt(o_buf[s, :, lanes(tp)], wd_ref[:, lanes(tp)])
-        for k in range(1, n_tp):
-            ag_arrival(s, k).wait_recv()
-            at = lanes(tp_peer(n_tp - k))
+
+        @pl.when(s > 0)
+        def _():
+            add_out(s - 1)
+
+        for k in range(1, line):
+            source = on_line(line - k) + side
+            al_copy(s, k, source).wait_recv()
+            ap_copy(s, k, source).start()
+            at = lanes(source)
+            gh[...] += mm_nt(o_buf[s, :, at], wd_ref[:, at])
+        for k in range(line):
+            source = on_line(line - k) + 1 - side
+            ap_copy(s, k, source).wait_recv()
+            at = lanes(source)
             gh[...] += mm_nt(o_buf[s, :, at], wd_ref[:, at])
 
         @pl.loop(1, n_cl)
@@ -206,9 +294,9 @@
         g_cli[0, s, cl] = gg
         g_cli[1, s, cl] = gu
 
-        @pl.loop(1, n_cl)
-        def _(k):
-            cg_copy(s, k, cl).start()
+        cg_near(s, 0, cl).start()
+        for m in range(1, pairs):
+            cg_far(s, m, cl).start()
 
         squares = sum_all(mm_nt(n_buf[s], n_buf[s]) * (mm_nt(gg, gg) + mm_nt(gu, gu)) + hh[s] * oo[...])
         sm_buf[s, tp, n_tp] = jnp.broadcast_to(squares, (1, dt))
@@ -234,10 +322,12 @@
         def _(k):
             sm_copy(s, k).start()
 
-        @pl.loop(1, n_tp)
-        def _(k):
-            rs_copy(s, k).wait_send()
-            ag_copy(s, k).wait_send()
+        for k in range(line):
+            rp_copy(s, k).wait_send()
+            ap_copy(s, k, tp).wait_send()
+        for k in range(1, line):
+            rl_copy(s, k).wait_send()
+            al_copy(s, k, tp).wait_send()
 
         @pl.loop(1, n_tp)
         def _(k):
@@ -250,12 +340,16 @@
         gain_square = jnp.sum(jnp.sum(gain_grad * gain_grad, axis=0), axis=1, keepdims=True)
         norm = jnp.sqrt(jnp.maximum(total[n_tp], 0.0) + gain_square + 1e-06)
         factor = jnp.where(total[n_tp + 1] < 0.5, limit / jnp.maximum(norm, limit), 0.0)
-        fin[cl, s] = factor
+        fin[s, cl, n_tp] = factor
         coef[s] = jnp.broadcast_to(factor[:, :tok] * (-LR), (1, tok))
         for p in range(n_tp):
             change = factor * gain_grad[p]
             gain[p] = gain[p] - LR * change
-            fin[cl, steps + p] = fin[cl, steps + p] + change
+            fin[s, cl, p] = change
+
+        @pl.loop(1, n_cl)
+        def _(k):
+            fi_copy(s, k, cl).start()
 
         @pl.loop(1, n_tp)
         def _(k):
@@ -267,49 +361,29 @@
 
     lax.fori_loop(0, steps, step, 0)
 
-    @pl.loop(1, n_cl)
-    def _(k):
-        fi_copy(k, cl).start()
+    forward(steps - 1)
+    add_out(steps - 1)
+    for i in range(q):
+        acc = jnp.zeros((1, dt), F32)
+        for s in range(steps):
+            for c in range(n_cl):
+                acc = acc + fin[s, c, cl * q + i]
+        ogain_ref[i] = acc * (1.0 / n_cl)
 
     @pl.loop(0, steps)
     def _(s):
         @pl.loop(1, n_cl)
         def _(k):
-            c = from_cl(k)
-            cn_copy(s, k, c).wait_recv()
-            ch_copy(s, k, c).wait_recv()
-            co_copy(s, k, c).wait_recv()
-            cg_copy(s, k, c).wait_recv()
             cn_copy(s, k, cl).wait_send()
-            ch_copy(s, k, cl).wait_send()
             co_copy(s, k, cl).wait_send()
-            cg_copy(s, k, cl).wait_send()
-
-    @pl.loop(1, n_cl)
-    def _(k):
-        fi_copy(k, from_cl(k)).wait_recv()
-        fi_copy(k, cl).wait_send()
-
-    for i in range(q):
-        acc = fin[0, steps + cl * q + i]
-        for c in range(1, n_cl):
-            acc = acc + fin[c, steps + cl * q + i]
-        ogain_ref[i] = acc * (1.0 / n_cl)
-
-    @pl.loop(0, n_cl)
-    def _(c):
-        @pl.loop(0, steps)
-        def _(s):
-            f = fin[c, s][:, :1] * (1.0 / n_cl)
-            n_cli[s, c] = (n_cli[s, c].astype(F32) * f).astype(BF16)
-            o_cli[s, c] = (o_cli[s, c].astype(F32) * f).astype(BF16)
-
-    rows = steps * n_cl * tok
-    ff = wg_ref.shape[1]
-    n_all = n_cli[...].reshape(rows, ds)
-    og_ref[...] = mm_tn(n_all, g_cli[0].reshape(rows, ff))
-    ou_ref[...] = mm_tn(n_all, g_cli[1].reshape(rows, ff))
-    od_ref[...] = mm_tn(h_cli[...].reshape(rows, ff), o_cli[...].reshape(rows, ds))
+            fi_copy(s, k, cl).wait_send()
+
+        for m in range(pairs):
+            ch_near(s, m, cl).wait_send()
+            cg_near(s, m, cl).wait_send()
+        for m in range(1, pairs):
+            ch_far(s, m, cl).wait_send()
+            cg_far(s, m, cl).wait_send()
 
 
 def on_device(n_tp, n_cl, inputs, targets, norm_gain, gate_weight, up_weight, down_weight, overflow):
@@ -318,6 +392,7 @@
     steps = overflow.shape[1]
     dt = width // n_tp
     ds = width // n_cl
+    line = n_tp // 2
     limit = 0.5 * math.sqrt(3.0 * width * ff * n_tp)
     flags = jnp.broadcast_to(overflow.astype(F32).reshape(steps, 1, 1), (steps, 1, dt))
     gain = norm_gain.reshape(n_tp, 1, dt)
@@ -338,14 +413,15 @@
             pltpu.VMEM((n_tp, 1, dt), F32),
             pltpu.VMEM((steps, tok, width), BF16),
             pltpu.VMEM((steps, tok, width), BF16),
-            pltpu.VMEM((n_tp, tok, dt), BF16),
-            pltpu.VMEM((steps, n_tp - 1, tok, dt), BF16),
+            pltpu.VMEM((2, line, tok, dt), BF16),
+            pltpu.VMEM((steps, line, tok, dt), BF16),
+            pltpu.VMEM((steps, line - 1, tok, dt), BF16),
             pltpu.VMEM((steps, n_tp, n_tp + 2, 1, dt), F32),
             pltpu.VMEM((steps, n_cl, tok, ds), BF16),
             pltpu.VMEM((steps, n_cl, tok, ds), BF16),
             pltpu.VMEM((steps, n_cl, tok, ff), BF16),
             pltpu.VMEM((2, steps, n_cl, tok, ff), BF16),
-            pltpu.VMEM((n_cl, steps + n_tp, 1, dt), F32),
+            pltpu.VMEM((steps, n_cl, n_tp + 1, 1, dt), F32),
             pltpu.VMEM((tok, ff), F32),
             pltpu.VMEM((tok, ff), F32),
             pltpu.VMEM((tok, ff), F32),
@@ -353,14 +429,16 @@
             pltpu.VMEM((steps, tok, tok), F32),
             pltpu.VMEM((tok, tok), F32),
             pltpu.VMEM((steps, 1, tok), F32),
-            dma((n_tp - 1,)), dma((steps, n_tp - 1)),
-            dma((n_tp - 1,)), dma((steps, n_tp - 1)),
+            dma((line,)), dma((steps, line)),
+            dma((line - 1,)), dma((steps, line - 1)),
+            dma((line,)), dma((steps, line)),
+            dma((line - 1,)), dma((steps, line - 1)),
             dma((n_tp - 1,)), dma((steps, n_tp - 1)),
             dma((steps, n_cl - 1)), dma((steps, n_cl - 1)),
             dma((steps, n_cl - 1)), dma((steps, n_cl - 1)),
             dma((steps, n_cl - 1)), dma((steps, n_cl - 1)),
             dma((steps, n_cl - 1)), dma((steps, n_cl - 1)),
-            dma((n_cl - 1,)), dma((n_cl - 1,)),
+            dma((steps, n_cl - 1)), dma((steps, n_cl - 1)),
         ],
         compiler_params=pltpu.CompilerParams(
             collective_id=0, has_side_effects=True, vmem_limit_bytes=48 * 1024 * 1024

time: 146 us -> 119 us (0.82); the launches traced: 145 us -> 119 us
  Pallas kernels: 137 us -> 111 us
    pallas_call x1, Pallas kernels: 137 us -> 111 us  [on_device(): pl.pallas_call(functools.partial(kernel, n_tp, n_cl, steps, limit), out_s...]
where the time goes in v2:
time: 119 us
  Pallas kernels  111 us (93%)
  local copies, waits for them, and re-layouts  6.34 us (5%)
    pallas_call x1, Pallas kernels, on_device(): pl.pallas_call(functools.partial(kernel, n_tp, n_cl, steps, limit), out_s...  111 us
    unnamed x10, local copies, waits for them, and re-layouts  6.27 us

profile of v2, /device:TPU:0, one launch (start us, length us, event | category | flops | bytes accessed | tf_op | source)
XLA Modules:
  0.0 119.0 jit_solution(5713595760228242461)
XLA Ops:
  0.6 0.7 convert_bitcast_fusion
  1.3 0.1 broadcast_in_dim.8.flag_ref
  1.4 0.0 copy-start
  1.4 1.0 copy-done
  2.4 0.0 copy-start.1
  2.4 1.0 copy-done.1
  3.4 0.0 copy-start.2
  3.5 0.7 copy-done.2
  4.1 111.4 %fedavg_round.1 = (f32[512,512]{1,0:T(8,128)S(1)}, f32[512,512]{1,0:T(8,128)S(1)}, f32[512,512]{1,0:T(8,128)S(1)}, f32[2,1,256]{2,1,0:T(1,128)S(1)}) custom-call(bf16[128,2048]{1,0:T(8,128)(2,1)S(1)} %bitcast.6, bf16[128,2048]{1,0:T(8,128)(2,1)S(1)} %bitcast.7, f32[8,1,256]{2,1,0:T(1,128)S(1)} %bitcast.8, bf16[2048,512]{1,0:T(8,128)(2,1)} %wg_ref.1, ...), custom_call_target="tpu_custom_call" | custom-call | tf_op jit(solution)/shard_map/fedavg_round/pallas_call | solution.py:401
  115.5 1.0 copy.15
  116.5 1.0 copy.16
  117.4 1.0 copy.17
  118.4 0.6 copy.18
Async XLA Ops:
  1.4 1.0 copy-start
  2.4 1.0 copy-start.1
  3.4 0.7 copy-start.2

commit v3 on v2

--- a/solution.py
+++ b/solution.py
@@ -32,10 +32,11 @@
 
 def kernel(
     n_tp, n_cl, steps, limit,
-    x_ref, t_ref, gain_ref, wg_ref, wu_ref, wd_ref, flag_ref,
+    x_ref, t_ref, gain_ref, wg_hbm, wu_hbm, wd_hbm, flag_ref,
     og_ref, ou_ref, od_ref, ogain_ref,
+    wg_ref, wu_ref, wd_ref, load, o_hist,
     scaled, gain, n_buf, o_buf, part, pair_buf, line_buf, sm_buf, n_cli, o_cli, h_cli, g_cli, fin,
-    ga, ua, sg, gh, hh, oo, coef,
+    ga, ua, sg, gh, nn, hh, oo, oh, coef,
     rp_s, rp_r, rl_s, rl_r, ap_s, ap_r, al_s, al_r, sm_s, sm_r,
     cn_s, cn_r, ch_s, ch_r, co_s, co_r, cg_s, cg_r, fi_s, fi_r,
 ):
@@ -52,6 +53,12 @@
     def cl_peer(k):
         return lax.rem(cl + k, n_cl)
 
+    loads = [
+        pltpu.make_async_copy(src, dst, load.at[i])
+        for i, (src, dst) in enumerate(((wg_hbm, wg_ref), (wu_hbm, wu_ref), (wd_hbm, wd_ref)))
+    ]
+    for copy in loads:
+        copy.start()
     barrier = pltpu.get_barrier_semaphore()
 
     @pl.loop(1, n_tp)
@@ -186,6 +193,24 @@
     og_ref[...] = jnp.zeros_like(og_ref)
     ou_ref[...] = jnp.zeros_like(ou_ref)
     od_ref[...] = jnp.zeros_like(od_ref)
+    past = steps - 1
+    rows = past * tok
+    ff = wg_ref.shape[1]
+    coef[...] = jnp.zeros_like(coef)
+    o_hist[...] = jnp.zeros_like(o_hist)
+    for j in range(past):
+        n_buf[j] = jnp.zeros((tok, width), BF16)
+        h_cli[j, cl] = jnp.zeros((tok, ff), BF16)
+        g_cli[0, j, cl] = jnp.zeros((tok, ff), BF16)
+        g_cli[1, j, cl] = jnp.zeros((tok, ff), BF16)
+    for copy in loads:
+        copy.wait()
+
+    def h_past():
+        return h_cli[:past, cl].reshape(rows, ff)
+
+    def g_past(i):
+        return g_cli[i, :past, cl].reshape(rows, ff)
 
     def step(s, carry):
         for p in range(n_tp):
@@ -204,29 +229,23 @@
         ga[...] = mm(normed, wg_ref[...])
         ua[...] = mm(normed, wu_ref[...])
 
-        @pl.loop(0, s)
-        def _(j):
-            p = (mm_nt(n_buf[s], n_buf[j]) * coef[j]).astype(BF16)
-            ga[...] += mm(p, g_cli[0, j, cl])
-            ua[...] += mm(p, g_cli[1, j, cl])
+        @pl.when(s > 0)
+        def _():
+            p = (mm_nt(n_buf[s], n_buf[:past].reshape(rows, width)) * coef[...]).astype(BF16)
+            ga[...] += mm(p, g_past(0))
+            ua[...] += mm(p, g_past(1))
 
         gate = ga[...]
         sig = jax.nn.sigmoid(gate)
         silu = gate * sig
         sg[...] = sig
-        h_cli[s, cl] = (silu * ua[...]).astype(BF16)
-
-        @pl.loop(0, s + 1)
-        def _(j):
-            hh[j] = mm_nt(h_cli[s, cl], h_cli[j, cl])
+        hidden = (silu * ua[...]).astype(BF16)
+        h_cli[s, cl] = hidden
+        p_h = (mm_nt(hidden, h_past()) * coef[...]).astype(BF16)
 
         def out_chunk(p):
-            first = mm(h_cli[s, cl], wd_ref[:, lanes(p)])
-
-            def more(j, acc):
-                return acc + mm((hh[j] * coef[j]).astype(BF16), o_buf[j, :, lanes(p)])
-
-            return lax.fori_loop(0, s, more, first)
+            at = lanes(p)
+            return mm(hidden, wd_ref[:, at]) + mm(p_h, o_hist[:, :, at].reshape(rows, dt))
 
         order = list(range(1, line)) + [0]
         for k in order:
@@ -249,6 +268,8 @@
         def _():
             forward(s - 1)
 
+        nn[...] = mm_nt(n_buf[s], n_buf[s])
+        hh[...] = mm_nt(h_cli[s, cl], h_cli[s, cl])
         for k in range(1, line):
             rl_copy(s, k).wait_recv()
             summed = summed + line_buf[s, k - 1].astype(F32)
@@ -258,37 +279,35 @@
         for k in range(1, line):
             al_copy(s, k, tp).start()
 
-        gh[...] = mm_nt(o_buf[s, :, lanes(tp)], wd_ref[:, lanes(tp)])
-
-        @pl.when(s > 0)
-        def _():
-            add_out(s - 1)
-
+        def arrived(p, first):
+            at = lanes(p)
+            block = o_buf[s, :, at]
+            for ref, value in (
+                (gh, mm_nt(block, wd_ref[:, at])),
+                (oo, mm_nt(block, block)),
+                (oh, mm_nt(block, o_hist[:, :, at].reshape(rows, dt))),
+            ):
+                ref[...] = value if first else ref[...] + value
+
+        arrived(tp, True)
         for k in range(1, line):
             source = on_line(line - k) + side
             al_copy(s, k, source).wait_recv()
             ap_copy(s, k, source).start()
-            at = lanes(source)
-            gh[...] += mm_nt(o_buf[s, :, at], wd_ref[:, at])
+            arrived(source, False)
         for k in range(line):
             source = on_line(line - k) + 1 - side
             ap_copy(s, k, source).wait_recv()
-            at = lanes(source)
-            gh[...] += mm_nt(o_buf[s, :, at], wd_ref[:, at])
+            arrived(source, False)
 
         @pl.loop(1, n_cl)
         def _(k):
             co_copy(s, k, cl).start()
 
-        @pl.loop(0, s)
-        def _(j):
-            p = (mm_nt(o_buf[s], o_buf[j]) * coef[j]).astype(BF16)
-            gh[...] += mm(p, h_cli[j, cl])
-
-        oo[...] = mm_nt(o_buf[s], o_buf[s])
         sig = sg[...]
         gate = ga[...]
-        grad_hidden = gh[...]
+        grad_hidden = gh[...] + mm((oh[...] * coef[...]).astype(BF16), h_past())
+        old_g, old_u = g_past(0), g_past(1)
         gg = (grad_hidden * ua[...] * (sig * (1.0 + gate * (1.0 - sig)))).astype(BF16)
         gu = (grad_hidden * (gate * sig)).astype(BF16)
         g_cli[0, s, cl] = gg
@@ -298,29 +317,24 @@
         for m in range(1, pairs):
             cg_far(s, m, cl).start()
 
-        squares = sum_all(mm_nt(n_buf[s], n_buf[s]) * (mm_nt(gg, gg) + mm_nt(gu, gu)) + hh[s] * oo[...])
+        squares = sum_all(nn[...] * (mm_nt(gg, gg) + mm_nt(gu, gu)) + hh[...] * oo[...])
         sm_buf[s, tp, n_tp] = jnp.broadcast_to(squares, (1, dt))
         sm_buf[s, tp, n_tp + 1] = flag_ref[s]
 
-        @pl.loop(0, s)
-        def _(j):
-            oo_j = mm_nt(g_cli[0, s, cl], g_cli[0, j, cl]) + mm_nt(g_cli[1, s, cl], g_cli[1, j, cl])
-            hh[j] = oo_j * coef[j]
-
-        @pl.loop(0, n_tp)
-        def _(p):
-            rows = pl.ds(pl.multiple_of(p * dt, dt), dt)
-            first = mm_nt(g_cli[0, s, cl], wg_ref[rows, :]) + mm_nt(g_cli[1, s, cl], wu_ref[rows, :])
-
-            def more(j, acc):
-                return acc + mm(hh[j].astype(BF16), n_buf[j, :, lanes(p)])
-
-            grad_normed = lax.fori_loop(0, s, more, first)
-            sm_buf[s, tp, p] = jnp.sum(grad_normed * scaled[:, lanes(p)], axis=0, keepdims=True)
+        p_g = ((mm_nt(gg, old_g) + mm_nt(gu, old_u)) * coef[...]).astype(BF16)
+        for p in range(n_tp):
+            at = slice(p * dt, (p + 1) * dt)
+            grad_normed = mm_nt(gg, wg_ref[at, :]) + mm_nt(gu, wu_ref[at, :])
+            grad_normed = grad_normed + mm(p_g, n_buf[:past, :, at].reshape(rows, dt))
+            sm_buf[s, tp, p] = jnp.sum(grad_normed * scaled[:, at], axis=0, keepdims=True)
 
         @pl.loop(1, n_tp)
         def _(k):
             sm_copy(s, k).start()
+
+        @pl.when(s > 0)
+        def _():
+            add_out(s - 1)
 
         for k in range(line):
             rp_copy(s, k).wait_send()
@@ -341,7 +355,12 @@
         norm = jnp.sqrt(jnp.maximum(total[n_tp], 0.0) + gain_square + 1e-06)
         factor = jnp.where(total[n_tp + 1] < 0.5, limit / jnp.maximum(norm, limit), 0.0)
         fin[s, cl, n_tp] = factor
-        coef[s] = jnp.broadcast_to(factor[:, :tok] * (-LR), (1, tok))
+
+        @pl.when(s < past)
+        def _():
+            coef[:, pl.ds(pl.multiple_of(s * tok, tok), tok)] = factor[:, :tok] * (-LR)
+            o_hist[s] = o_buf[s]
+
         for p in range(n_tp):
             change = factor * gain_grad[p]
             gain[p] = gain[p] - LR * change
@@ -406,9 +425,14 @@
             jax.ShapeDtypeStruct((ff, ds), F32),
             jax.ShapeDtypeStruct((ds // dt, 1, dt), F32),
         ),
-        in_specs=[vmem] * 7,
+        in_specs=[vmem] * 3 + [pl.BlockSpec(memory_space=pl.ANY)] * 3 + [vmem],
         out_specs=(vmem,) * 4,
         scratch_shapes=[
+            pltpu.VMEM((width, ff), BF16),
+            pltpu.VMEM((width, ff), BF16),
+            pltpu.VMEM((ff, width), BF16),
+            dma((3,)),
+            pltpu.VMEM((steps - 1, tok, width), BF16),
             pltpu.VMEM((tok, width), F32),
             pltpu.VMEM((n_tp, 1, dt), F32),
             pltpu.VMEM((steps, tok, width), BF16),
@@ -426,9 +450,11 @@
             pltpu.VMEM((tok, ff), F32),
             pltpu.VMEM((tok, ff), F32),
             pltpu.VMEM((tok, ff), F32),
-            pltpu.VMEM((steps, tok, tok), F32),
             pltpu.VMEM((tok, tok), F32),
-            pltpu.VMEM((steps, 1, tok), F32),
+            pltpu.VMEM((tok, tok), F32),
+            pltpu.VMEM((tok, tok), F32),
+            pltpu.VMEM((tok, (steps - 1) * tok), F32),
+            pltpu.VMEM((1, (steps - 1) * tok), F32),
             dma((line,)), dma((steps, line)),
             dma((line - 1,)), dma((steps, line - 1)),
             dma((line,)), dma((steps, line)),
@@ -441,7 +467,7 @@
             dma((steps, n_cl - 1)), dma((steps, n_cl - 1)),
         ],
         compiler_params=pltpu.CompilerParams(
-            collective_id=0, has_side_effects=True, vmem_limit_bytes=48 * 1024 * 1024
+            collective_id=0, has_side_effects=True, vmem_limit_bytes=58 * 1024 * 1024
         ),
         name="fedavg_round",
     )(inputs[0], targets[0], gain, gate_weight, up_weight, down_weight, flags)

time: 119 us -> 111 us (0.933)
  Pallas kernels: 111 us -> 104 us
    pallas_call x1, Pallas kernels: 111 us -> 104 us  [on_device(): pl.pallas_call(functools.partial(kernel, n_tp, n_cl, steps, limit), out_s...]
    unnamed x10, local copies, waits for them, and re-layouts: 6.27 us -> 4.94 us
where the time goes in v3:
time: 111 us
  Pallas kernels  104 us (94%)
  local copies, waits for them, and re-layouts  5.59 us (5%)
    pallas_call x1, Pallas kernels, on_device(): pl.pallas_call(functools.partial(kernel, n_tp, n_cl, steps, limit), out_s...  104 us
    unnamed x10, local copies, waits for them, and re-layouts  4.94 us

profile of v3, /device:TPU:0, one launch (start us, length us, event | category | flops | bytes accessed | tf_op | source)
XLA Modules:
  0.0 110.7 jit_solution(149613654803620013)
XLA Ops:
  0.6 0.7 convert_bitcast_fusion
  1.3 0.7 broadcast_in_dim.8.flag_ref
  1.9 103.7 %fedavg_round.1 = (f32[512,512]{1,0:T(8,128)}, f32[512,512]{1,0:T(8,128)}, f32[512,512]{1,0:T(8,128)}, f32[2,1,256]{2,1,0:T(1,128)}) custom-call(bf16[128,2048]{1,0:T(8,128)(2,1)} %bitcast.6, bf16[128,2048]{1,0:T(8,128)(2,1)} %bitcast.7, f32[8,1,256]{2,1,0:T(1,128)} %bitcast.8, bf16[2048,512]{1,0:T(8,128)(2,1)} %wg_hbm.1, bf16[2048,512]{1,0:T(8,128)(2,1)} %wu_hbm.1, ...), custom_call_target="tpu_custom_call" | custom-call | tf_op jit(solution)/shard_map/fedavg_round/pallas_call | solution.py:420
  105.7 0.0 copy-start.1
  105.7 0.0 copy-start
  105.7 2.4 %copy.15 = f32[512,512]{1,0:T(8,128)} copy(f32[512,512]{1,0:T(8,128)} %get-tuple-element.16) | data formatting | bytes 2097152
  108.1 0.0 copy-done.1
  108.1 0.0 copy-start.2
  108.1 1.0 copy.16
  109.1 0.0 copy-done
  109.1 1.0 copy.17
  110.1 0.0 copy-done.2
  110.1 0.6 copy.18
Async XLA Ops:
  105.7 2.4 %copy-start.1 = (f32[512,512]{1,0:T(8,128)S(1)}, f32[512,512]{1,0:T(8,128)}, u32[]{:S(2)}) copy-start(f32[512,512]{1,0:T(8,128)} %get-tuple-element.17) | copy-start | bytes 3145732
  105.7 3.4 %copy-start = (f32[512,512]{1,0:T(8,128)S(1)}, f32[512,512]{1,0:T(8,128)}, u32[]{:S(2)}) copy-start(f32[512,512]{1,0:T(8,128)} %get-tuple-element.18) | copy-start | bytes 3145732
  108.1 1.9 %copy-start.2 = (f32[2,1,256]{2,1,0:T(1,128)S(1)}, f32[2,1,256]{2,1,0:T(1,128)}, u32[]{:S(2)}) copy-start(f32[2,1,256]{2,1,0:T(1,128)} %get-tuple-element.11) | copy-start | bytes 6148

commit v4 on v3

--- a/solution.py
+++ b/solution.py
@@ -319,7 +319,7 @@
 
         squares = sum_all(nn[...] * (mm_nt(gg, gg) + mm_nt(gu, gu)) + hh[...] * oo[...])
         sm_buf[s, tp, n_tp] = jnp.broadcast_to(squares, (1, dt))
-        sm_buf[s, tp, n_tp + 1] = flag_ref[s]
+        sm_buf[s, tp, n_tp + 1] = jnp.full((1, dt), flag_ref[s], jnp.int32).astype(F32)
 
         p_g = ((mm_nt(gg, old_g) + mm_nt(gu, old_u)) * coef[...]).astype(BF16)
         for p in range(n_tp):
@@ -335,6 +335,17 @@
         @pl.when(s > 0)
         def _():
             add_out(s - 1)
+
+        n_cli[s, cl] = n_buf[s, :, slice_of(cl)]
+        o_cli[s, cl] = o_buf[s, :, slice_of(cl)]
+
+        @pl.when(s < past)
+        def _():
+            o_hist[s] = o_buf[s]
+
+        @pl.when(s == past)
+        def _():
+            forward(s)
 
         for k in range(line):
             rp_copy(s, k).wait_send()
@@ -359,7 +370,6 @@
         @pl.when(s < past)
         def _():
             coef[:, pl.ds(pl.multiple_of(s * tok, tok), tok)] = factor[:, :tok] * (-LR)
-            o_hist[s] = o_buf[s]
 
         for p in range(n_tp):
             change = factor * gain_grad[p]
@@ -374,13 +384,10 @@
         def _(k):
             sm_copy(s, k).wait_send()
 
-        n_cli[s, cl] = n_buf[s, :, slice_of(cl)]
-        o_cli[s, cl] = o_buf[s, :, slice_of(cl)]
         return carry
 
     lax.fori_loop(0, steps, step, 0)
 
-    forward(steps - 1)
     add_out(steps - 1)
     for i in range(q):
         acc = jnp.zeros((1, dt), F32)
@@ -413,7 +420,6 @@
     ds = width // n_cl
     line = n_tp // 2
     limit = 0.5 * math.sqrt(3.0 * width * ff * n_tp)
-    flags = jnp.broadcast_to(overflow.astype(F32).reshape(steps, 1, 1), (steps, 1, dt))
     gain = norm_gain.reshape(n_tp, 1, dt)
     dma = pltpu.SemaphoreType.DMA
     vmem = pl.BlockSpec(memory_space=pltpu.VMEM)
@@ -425,7 +431,8 @@
             jax.ShapeDtypeStruct((ff, ds), F32),
             jax.ShapeDtypeStruct((ds // dt, 1, dt), F32),
         ),
-        in_specs=[vmem] * 3 + [pl.BlockSpec(memory_space=pl.ANY)] * 3 + [vmem],
+        in_specs=[vmem] * 3 + [pl.BlockSpec(memory_space=pl.ANY)] * 3
+        + [pl.BlockSpec(memory_space=pltpu.SMEM)],
         out_specs=(vmem,) * 4,
         scratch_shapes=[
             pltpu.VMEM((width, ff), BF16),
@@ -470,7 +477,7 @@
             collective_id=0, has_side_effects=True, vmem_limit_bytes=58 * 1024 * 1024
         ),
         name="fedavg_round",
-    )(inputs[0], targets[0], gain, gate_weight, up_weight, down_weight, flags)
+    )(inputs[0], targets[0], gain, gate_weight, up_weight, down_weight, overflow.reshape(steps))
     return gate, up, down, gain_out.reshape(ds)
 
 

time: 111 us -> 109 us (0.982)
  no operation moved by 1% of the time
where the time goes in v4:
time: 109 us
  Pallas kernels  104 us (95%)
  local copies, waits for them, and re-layouts  4.94 us (5%)
    pallas_call x1, Pallas kernels, on_device(): pl.pallas_call(functools.partial(kernel, n_tp, n_cl, steps, limit), out_s...  104 us
    unnamed x10, local copies, waits for them, and re-layouts  4.94 us

profile of v4, /device:TPU:0, one launch (start us, length us, event | category | flops | bytes accessed | tf_op | source)
XLA Modules:
  0.0 109.3 jit_solution(8910616028785070034)
XLA Ops:
  0.6 103.7 %fedavg_round.1 = (f32[512,512]{1,0:T(8,128)}, f32[512,512]{1,0:T(8,128)}, f32[512,512]{1,0:T(8,128)}, f32[2,1,256]{2,1,0:T(1,128)}) custom-call(bf16[128,2048]{1,0:T(8,128)(2,1)} %bitcast.5, bf16[128,2048]{1,0:T(8,128)(2,1)} %bitcast.6, f32[8,1,256]{2,1,0:T(1,128)} %bitcast.7, bf16[2048,512]{1,0:T(8,128)(2,1)} %wg_hbm.1, bf16[2048,512]{1,0:T(8,128)(2,1)} %wu_hbm.1, ...), custom_call_target="tpu_custom_call" | custom-call | tf_op jit(solution)/shard_map/fedavg_round/pallas_call | solution.py:426
  104.4 0.0 copy-start.1
  104.4 0.0 copy-start
  104.4 2.4 %copy.15 = f32[512,512]{1,0:T(8,128)} copy(f32[512,512]{1,0:T(8,128)} %get-tuple-element.16) | data formatting | bytes 2097152
  106.8 0.0 copy-done.1
  106.8 0.0 copy-start.2
  106.8 1.0 copy.16
  107.8 0.0 copy-done
  107.8 1.0 copy.17
  108.7 0.0 copy-done.2
  108.7 0.6 copy.18
Async XLA Ops:
  104.4 2.4 %copy-start.1 = (f32[512,512]{1,0:T(8,128)S(1)}, f32[512,512]{1,0:T(8,128)}, u32[]{:S(2)}) copy-start(f32[512,512]{1,0:T(8,128)} %get-tuple-element.17) | copy-start | bytes 3145732
  104.4 3.4 %copy-start = (f32[512,512]{1,0:T(8,128)S(1)}, f32[512,512]{1,0:T(8,128)}, u32[]{:S(2)}) copy-start(f32[512,512]{1,0:T(8,128)} %get-tuple-element.18) | copy-start | bytes 3145732
  106.8 1.9 %copy-start.2 = (f32[2,1,256]{2,1,0:T(1,128)S(1)}, f32[2,1,256]{2,1,0:T(1,128)}, u32[]{:S(2)}) copy-start(f32[2,1,256]{2,1,0:T(1,128)} %get-tuple-element.11) | copy-start | bytes 6148
